TPU v7x, 32 devices: a whole 2x2x4 slice. The times are simulated.
32 devices in a mesh: section: 2 (over core), batch: 4 (over y, x), rows: 4 (over z).
Axes of the slice: x: 2, y: 2, z: 4, core: 2. Of those that a mesh axis runs over, the one named last changes fastest.
Arguments:
- frames: float32 [32, 12, 16, 64], P(('section', 'batch'), None, 'rows'), may hold values from -32 to 32
- counts: int32 [32], P(('section', 'batch')), may hold values from 1 to 4
- cell_mask: int32 [32, 16, 64], P(('section', 'batch'), 'rows'), may hold values 0 or 1
- step_index: int32 [32], P(('section', 'batch')), may hold values from 0 to 3
- lift_weight: float32 [12, 128], replicated, may hold values from -1.75 to 1.75
- lift_bias: float32 [128], replicated, may hold values from -3 to 3
- enc_norm1_gain: float32 [128], replicated, may hold values from 0.25 to 1.75
- enc_norm1_bias: float32 [128], replicated, may hold values from -3 to 3
- enc_conv1: float32 [3, 3, 128, 128], replicated, may hold values from -0.1875 to 0.1875
- enc_step_table: float32 [4, 256], replicated, may hold values from -2 to 2
- enc_norm2_gain: float32 [128], replicated, may hold values from 0.25 to 1.75
- enc_norm2_bias: float32 [128], replicated, may hold values from -3 to 3
- enc_conv2: float32 [3, 3, 128, 128], replicated, may hold values from -0.1875 to 0.1875
- enc_conv2_bias: float32 [128], replicated, may hold values from -3 to 3
- reducer_weight: float32 [2, 2, 128, 128], replicated, may hold values from -0.25 to 0.25
- reducer_bias: float32 [128], replicated, may hold values from -3 to 3
- up_weight: float32 [2, 2, 128, 128], replicated, may hold values from -0.5 to 0.5
- up_bias: float32 [128], replicated, may hold values from -3 to 3
- dec_norm1_gain: float32 [256], replicated, may hold values from 0.25 to 1.75
- dec_norm1_bias: float32 [256], replicated, may hold values from -3 to 3
- dec_conv1: float32 [3, 3, 256, 128], replicated, may hold values from -0.125 to 0.125
- dec_step_table: float32 [4, 256], replicated, may hold values from -2 to 2
- dec_norm2_gain: float32 [128], replicated, may hold values from 0.25 to 1.75
- dec_norm2_bias: float32 [128], replicated, may hold values from -3 to 3
- dec_conv2: float32 [3, 3, 128, 128], replicated, may hold values from -0.1875 to 0.1875
- dec_conv2_bias: float32 [128], replicated, may hold values from -3 to 3
- skip_weight: float32 [256, 128], replicated, may hold values from -0.375 to 0.375
- skip_bias: float32 [128], replicated, may hold values from -3 to 3
- cotangent: float32 [32, 16, 64, 128], P(('section', 'batch'), 'rows'), may hold values from -6 to 6
Outputs:
- output: float32 [32, 16, 64, 128], P(('section', 'batch'), 'rows')
- frames_grad: float32 [32, 12, 16, 64], P(('section', 'batch'), None, 'rows')
- grad_lift_weight: float32 [12, 128], replicated
- grad_lift_bias: float32 [128], replicated
- grad_enc_norm1_gain: float32 [128], replicated
- grad_enc_norm1_bias: float32 [128], replicated
- grad_enc_conv1: float32 [3, 3, 128, 128], replicated
- grad_enc_step_table: float32 [4, 256], replicated
- grad_enc_norm2_gain: float32 [128], replicated
- grad_enc_norm2_bias: float32 [128], replicated
- grad_enc_conv2: float32 [3, 3, 128, 128], replicated
- grad_enc_conv2_bias: float32 [128], replicated
- grad_down_weight: float32 [2, 2, 128, 128], replicated
- grad_down_bias: float32 [128], replicated
- grad_up_weight: float32 [2, 2, 128, 128], replicated
- grad_up_bias: float32 [128], replicated
- grad_dec_norm1_gain: float32 [256], replicated
- grad_dec_norm1_bias: float32 [256], replicated
- grad_dec_conv1: float32 [3, 3, 256, 128], replicated
- grad_dec_step_table: float32 [4, 256], replicated
- grad_dec_norm2_gain: float32 [128], replicated
- grad_dec_norm2_bias: float32 [128], replicated
- grad_dec_conv2: float32 [3, 3, 128, 128], replicated
- grad_dec_conv2_bias: float32 [128], replicated
- grad_skip_weight: float32 [256, 128], replicated
- grad_skip_bias: float32 [128], replicated
All inputs are finite; a program needn't handle non-finite values. No bound on the sum of `cell_mask` on one device may be relied on, other than what follows from the above.
Results may differ from a plain program's by a relative error of at most 0.0003.
Values sent between devices are 32-bit elements; how exact they have to be, the bound alone decides.
A program may use at most 128 MiB of HBM per device.

v0:
```python
import functools
from types import SimpleNamespace
from typing import Any, NamedTuple

import jax
import jax.numpy as jnp
from jax import lax
from jax.experimental import pallas as pl
from jax.experimental.pallas import tpu as pltpu
from jax.sharding import PartitionSpec as P

GROUPS = 8
FIELDS = 3
HIST = 4


EPS = 1e-05
HIGH = lax.Precision.HIGHEST


def extended(cells, sides, width):
    for axis, dim in sides:
        count = lax.axis_size(axis)
        ends = count - 1
        head = lax.slice_in_dim(cells, 0, width, axis=dim)
        tail = lax.slice_in_dim(cells, cells.shape[dim] - width, cells.shape[dim], axis=dim)
        cells = jnp.concatenate(
            [
                lax.ppermute(tail, axis, [(i, (i + 1) % count) for i in range(ends)]),
                cells,
                lax.ppermute(head, axis, [((i + 1) % count, i) for i in range(ends)]),
            ],
            axis=dim,
        )
    return cells


def from_behind(value, axis, steps):
    count = lax.axis_size(axis)
    pairs = [(source, (source + steps) % count) for source in range(count)]
    return lax.ppermute(value, axis, pairs)


def group_view(value_arrays):
    extent = value_arrays.shape
    return value_arrays.reshape(extent[:-1] + (GROUPS, extent[-1] // GROUPS))


def global_sums(value_arrays):
    grouped = group_view(value_arrays)
    flat = grouped.reshape(-1, GROUPS, grouped.shape[-1])
    first_sum = jnp.sum(flat, axis=(0, 2))
    second_sum = jnp.sum(flat * flat, axis=(0, 2))
    return lax.psum((first_sum, second_sum), "rows")


def apply_norm(value_arrays, sum_one, sum_two, norm_gain, norm_bias, total):
    grouped = group_view(value_arrays)
    group_mean = sum_one / total
    variance = sum_two / total - group_mean * group_mean
    inverse = lax.rsqrt(variance + EPS)
    normed = (grouped - group_mean[:, None]) * inverse[:, None]
    return normed.reshape(value_arrays.shape) * norm_gain + norm_bias


def norm_back(value_arrays, grad_one, grad_two):
    grouped = group_view(value_arrays)
    extra = grad_one[:, None] + 2.0 * grouped * grad_two[:, None]
    return extra.reshape(value_arrays.shape)


def reduce_grads(grad_one, grad_two):
    return lax.psum((grad_one, grad_two), "rows")


def conv_rows(padded, kernel):
    widened = jnp.pad(padded, ((0, 0), (1, 1), (0, 0)))
    return lax.conv_general_dilated(
        widened[None],
        kernel,
        (1, 1),
        "VALID",
        dimension_numbers=("NHWC", "HWIO", "NHWC"),
        precision=HIGH,
    )[0]


def flipped(kernel):
    return jnp.transpose(kernel[::-1, ::-1], (0, 1, 3, 2))


def pad_grads(value_arrays):
    return extended(value_arrays, (("rows", 0),), 1)


def totals_of(inputs, conv1):
    strip = inputs.shape[0]
    cells = strip * lax.axis_size("rows") * inputs.shape[1]
    return (cells * (inputs.shape[2] // GROUPS), cells * (conv1.shape[3] // GROUPS))


def block_forward(inputs, weights, scale_part, shift_part):
    norm1_gain, norm1_bias, conv1, norm2_gain, norm2_bias, conv2, conv2_bias = weights
    total_in, total_mid = totals_of(inputs, conv1)
    sums_in = global_sums(inputs)

    def pad_rows(value_arrays):
        return extended(value_arrays, (("rows", 0),), 1)

    act_one = pad_rows(
        jax.nn.gelu(
            apply_norm(inputs, sums_in[0], sums_in[1], norm1_gain, norm1_bias, total_in),
            approximate=False,
        )
    )
    middle = conv_rows(act_one, conv1)
    sums_mid = global_sums(middle)
    shaped = (
        apply_norm(middle, sums_mid[0], sums_mid[1], norm2_gain, norm2_bias, total_mid)
        * (1.0 + scale_part)
        + shift_part
    )
    act_two = pad_rows(jax.nn.gelu(shaped, approximate=False))
    branch = conv_rows(act_two, conv2) + conv2_bias
    return (branch, (sums_in[0], sums_in[1], act_one, middle, sums_mid[0], sums_mid[1], act_two))


def block_backward(inputs, weights, scale_part, shift_part, kept, grad_out):
    norm1_gain, norm1_bias, conv1, norm2_gain, norm2_bias, conv2, conv2_bias = weights
    in_one, in_two, act_one, middle, mid_one, mid_two, act_two = kept
    total_in, total_mid = totals_of(inputs, conv1)
    grad_conv2 = jax.vjp(lambda kernel: conv_rows(act_two, kernel), conv2)[1](grad_out)[0]
    grad_bias2 = jnp.sum(grad_out, axis=(0, 1))
    grad_act_two = conv_rows(pad_grads(grad_out), flipped(conv2))

    def second_piece(middle_in, sum_one, sum_two, gain_in, incoming_bias, scale_in, shift_in):
        shaped = (
            apply_norm(middle_in, sum_one, sum_two, gain_in, incoming_bias, total_mid)
            * (1.0 + scale_in)
            + shift_in
        )
        return jax.nn.gelu(shaped, approximate=False)

    second_pull = jax.vjp(
        second_piece, middle, mid_one, mid_two, norm2_gain, norm2_bias, scale_part, shift_part
    )[1](grad_act_two)
    summed_one, summed_two = reduce_grads(second_pull[1], second_pull[2])
    grad_middle = second_pull[0] + norm_back(middle, summed_one, summed_two)
    grad_conv1 = jax.vjp(lambda kernel: conv_rows(act_one, kernel), conv1)[1](grad_middle)[0]
    grad_act_one = conv_rows(pad_grads(grad_middle), flipped(conv1))

    def first_piece(inputs_in, sum_one, sum_two, gain_in, incoming_bias):
        return jax.nn.gelu(
            apply_norm(inputs_in, sum_one, sum_two, gain_in, incoming_bias, total_in),
            approximate=False,
        )

    first_pull = jax.vjp(first_piece, inputs, in_one, in_two, norm1_gain, norm1_bias)[1](
        grad_act_one
    )
    first_one, first_two = reduce_grads(first_pull[1], first_pull[2])
    grad_inputs = first_pull[0] + norm_back(inputs, first_one, first_two)
    grads = (
        first_pull[3],
        first_pull[4],
        grad_conv1,
        second_pull[3],
        second_pull[4],
        grad_conv2,
        grad_bias2,
    )
    return (grad_inputs, grads, second_pull[5], second_pull[6])


def conditioning(step_item, table):
    one_hot = (jnp.arange(table.shape[0], dtype=jnp.int32) == step_item).astype(jnp.float32)
    condition = jnp.dot(one_hot, table, precision=HIGH)
    half_width = table.shape[1] // 2
    return (condition[:half_width], condition[half_width:], one_hot)


def project_in(frames_item, mask_item, count_item, incoming_weight, incoming_bias):
    history = jnp.arange(HIST, dtype=jnp.int32) >= HIST - count_item
    keep = jnp.repeat(history, FIELDS).astype(jnp.float32)
    lifted = (
        jnp.einsum(
            "fhw,fc->hwc", frames_item * keep[:, None, None], incoming_weight, precision=HIGH
        )
        + incoming_bias
    )
    return lifted * mask_item[:, :, None].astype(jnp.float32)


def coarsen_field(value_arrays, incoming_weight, incoming_bias):
    rows_here, width_here, depth_here = value_arrays.shape
    blocks = value_arrays.reshape(rows_here // 2, 2, width_here // 2, 2, depth_here)
    return jnp.einsum("iajbk,abkc->ijc", blocks, incoming_weight, precision=HIGH) + incoming_bias


def upsample(value_arrays, incoming_weight, incoming_bias):
    result = jnp.einsum("ijk,abkc->iajbc", value_arrays, incoming_weight, precision=HIGH)
    extent = result.shape
    return result.reshape(extent[0] * 2, extent[2] * 2, extent[4]) + incoming_bias


def flatten_all(pieces):
    return jnp.concatenate([piece.reshape(-1) for piece in pieces])


def unflatten_all(flat, templates):
    pieces = []
    offset_at = 0
    for template in templates:
        count_here = template.size
        pieces.append(flat[offset_at : offset_at + count_here].reshape(template.shape))
        offset_at += count_here
    return tuple(pieces)


def strips_body(
    frames,
    counts,
    cell_mask,
    step_index,
    lift_weight,
    lift_bias,
    enc_norm1_gain,
    enc_norm1_bias,
    enc_conv1,
    enc_step_table,
    enc_norm2_gain,
    enc_norm2_bias,
    enc_conv2,
    enc_conv2_bias,
    reducer_weight,
    reducer_bias,
    up_weight,
    up_bias,
    dec_norm1_gain,
    dec_norm1_bias,
    dec_conv1,
    dec_step_table,
    dec_norm2_gain,
    dec_norm2_bias,
    dec_conv2,
    dec_conv2_bias,
    skip_weight,
    skip_bias,
    cotangent,
):
    enc_weights = (
        enc_norm1_gain,
        enc_norm1_bias,
        enc_conv1,
        enc_norm2_gain,
        enc_norm2_bias,
        enc_conv2,
        enc_conv2_bias,
    )
    dec_weights = (
        dec_norm1_gain,
        dec_norm1_bias,
        dec_conv1,
        dec_norm2_gain,
        dec_norm2_bias,
        dec_conv2,
        dec_conv2_bias,
    )
    params = (
        lift_weight,
        lift_bias,
        enc_norm1_gain,
        enc_norm1_bias,
        enc_conv1,
        enc_step_table,
        enc_norm2_gain,
        enc_norm2_bias,
        enc_conv2,
        enc_conv2_bias,
        reducer_weight,
        reducer_bias,
        up_weight,
        up_bias,
        dec_norm1_gain,
        dec_norm1_bias,
        dec_conv1,
        dec_step_table,
        dec_norm2_gain,
        dec_norm2_bias,
        dec_conv2,
        dec_conv2_bias,
        skip_weight,
        skip_bias,
    )

    def forward_micro(carry, sliced):
        frames_item, mask_item, count_item, step_item = sliced
        lifted = project_in(frames_item, mask_item, count_item, lift_weight, lift_bias)
        enc_scale, enc_shift, unused_hot = conditioning(step_item, enc_step_table)
        enc_branch, enc_kept = block_forward(lifted, enc_weights, enc_scale, enc_shift)
        encoder_result = lifted + enc_branch
        coarse_field = coarsen_field(encoder_result, reducer_weight, reducer_bias)
        foreign = from_behind(coarse_field, "section", 1)
        raised_foreign = upsample(foreign, up_weight, up_bias)
        raised = from_behind(raised_foreign, "section", 1)
        joined = jnp.concatenate([raised, encoder_result], axis=-1)
        dec_scale, dec_shift, unused_again = conditioning(step_item, dec_step_table)
        dec_branch, dec_kept = block_forward(joined, dec_weights, dec_scale, dec_shift)
        output_item = jnp.dot(joined, skip_weight, precision=HIGH) + skip_bias + dec_branch
        return (carry, (output_item, (lifted, enc_kept, encoder_result, foreign, joined, dec_kept)))

    unused, (output, kept_all) = lax.scan(
        forward_micro, jnp.zeros((), jnp.float32), (frames, cell_mask, counts, step_index)
    )

    def backward_micro(totals, sliced):
        frames_item, mask_item, count_item, step_item, grad_out, kept = sliced
        lifted, enc_kept, encoder_result, foreign, joined, dec_kept = kept
        dec_scale, dec_shift, one_hot = conditioning(step_item, dec_step_table)
        grad_joined, dec_grads, dec_gscale, dec_gshift = block_backward(
            joined, dec_weights, dec_scale, dec_shift, dec_kept, grad_out
        )
        grad_skip_weight = jnp.einsum("hwk,hwc->kc", joined, grad_out, precision=HIGH)
        grad_skip_bias = jnp.sum(grad_out, axis=(0, 1))
        grad_joined = grad_joined + jnp.dot(grad_out, skip_weight.T, precision=HIGH)
        half_width = joined.shape[-1] // 2
        grad_raised = grad_joined[..., :half_width]
        grad_encoded = grad_joined[..., half_width:]
        grad_foreign_up = from_behind(grad_raised, "section", 1)
        up_pull = jax.vjp(upsample, foreign, up_weight, up_bias)[1](grad_foreign_up)
        coarse_gradient = from_behind(up_pull[0], "section", 1)
        reducer_pullback = jax.vjp(coarsen_field, encoder_result, reducer_weight, reducer_bias)[1](
            coarse_gradient
        )
        grad_encoded = grad_encoded + reducer_pullback[0]
        enc_scale, enc_shift, enc_hot = conditioning(step_item, enc_step_table)
        grad_lifted, enc_grads, enc_gscale, enc_gshift = block_backward(
            lifted, enc_weights, enc_scale, enc_shift, enc_kept, grad_encoded
        )
        grad_lifted = grad_lifted + grad_encoded
        proj_pull = jax.vjp(
            lambda frames_in, incoming_weight, incoming_bias: project_in(
                frames_in, mask_item, count_item, incoming_weight, incoming_bias
            ),
            frames_item,
            lift_weight,
            lift_bias,
        )[1](grad_lifted)
        enc_table_grad = enc_hot[:, None] * jnp.concatenate([enc_gscale, enc_gshift])[None, :]
        dec_table_grad = one_hot[:, None] * jnp.concatenate([dec_gscale, dec_gshift])[None, :]
        micro_list = (
            proj_pull[1],
            proj_pull[2],
            enc_grads[0],
            enc_grads[1],
            enc_grads[2],
            enc_table_grad,
            enc_grads[3],
            enc_grads[4],
            enc_grads[5],
            enc_grads[6],
            reducer_pullback[1],
            reducer_pullback[2],
            up_pull[1],
            up_pull[2],
            dec_grads[0],
            dec_grads[1],
            dec_grads[2],
            dec_table_grad,
            dec_grads[3],
            dec_grads[4],
            dec_grads[5],
            dec_grads[6],
            grad_skip_weight,
            grad_skip_bias,
        )
        micro_flat = flatten_all(micro_list)
        return (totals + micro_flat, proj_pull[0])

    total_size = sum((piece.size for piece in params))
    start_totals = jnp.zeros((total_size,), jnp.float32)
    flat_totals, frames_grad = lax.scan(
        backward_micro,
        start_totals,
        (frames, cell_mask, counts, step_index, cotangent, kept_all),
        reverse=True,
    )
    flat_totals = lax.psum(flat_totals, ("section", "batch", "rows"))
    grads = unflatten_all(flat_totals, params)
    return (output, frames_grad) + grads


F32 = jnp.float32
BF16 = jnp.bfloat16
MESH = pl.DeviceIdType.MESH
NN = ((1,), (0,))
NT = ((1,), (1,))
TN = ((0,), (0,))
HIGH_AT = (0, 2, 1)
LOW_AT = (4, 3, 5)
CHUNK = 512
class Given(NamedTuple):
    frames: Any
    counts: Any
    cell_mask: Any
    step_index: Any
    lift_weight: Any
    lift_bias: Any
    enc_norm1_gain: Any
    enc_norm1_bias: Any
    enc_conv1: Any
    enc_step_table: Any
    enc_norm2_gain: Any
    enc_norm2_bias: Any
    enc_conv2: Any
    enc_conv2_bias: Any
    reducer_weight: Any
    reducer_bias: Any
    up_weight: Any
    up_bias: Any
    dec_norm1_gain: Any
    dec_norm1_bias: Any
    dec_conv1: Any
    dec_step_table: Any
    dec_norm2_gain: Any
    dec_norm2_bias: Any
    dec_conv2: Any
    dec_conv2_bias: Any
    skip_weight: Any
    skip_bias: Any
    cotangent: Any


ARGUMENTS = Given._fields
LARGE = tuple(
    dict(
        dec_conv1=0,
        up_weight=0,
        reducer_weight=0,
        dec_conv2=0,
        skip_weight=0,
        enc_conv1=0,
        enc_conv2=0,
    )
)
IN_HBM = tuple(dict(frames=0, cell_mask=0, cotangent=0)) + LARGE
IN_SMEM = tuple(dict(counts=0, step_index=0))
LATE = 64
SMALL_ROWS = dict(
    enc_conv2_bias=(0, 1),
    reducer_bias=(1, 1),
    up_bias=(2, 1),
    dec_conv2_bias=(3, 1),
    skip_bias=(3, 1),
    dec_norm1_gain=(4, 2),
    dec_norm1_bias=(6, 2),
    dec_norm2_gain=(8, 1),
    dec_norm2_bias=(9, 1),
    dec_step_table=(16, 8),
    lift_weight=(LATE, 12),
    lift_bias=(LATE + 12, 1),
    enc_norm1_gain=(LATE + 16, 1),
    enc_norm1_bias=(LATE + 17, 1),
    enc_norm2_gain=(LATE + 18, 1),
    enc_norm2_bias=(LATE + 19, 1),
    enc_step_table=(LATE + 24, 8),
)
LATE_COUNT = 32
PIECES = 1
SMALL_COUNT = LATE + LATE_COUNT
DUE = ((), (), (), (), (), (0,), (), (1,), (), (), (2,), (3, 0), (), (), (1,), (), (), (2,), (0,), (1, 4, 3), (2,), (), (), (5, 0), (1, 3), (4, 2), (), (6,), (7, 3, 0, 5, 4, 1, 2))
REST = (6, 3, 7, 4, 5, 6, 8, 7, 0, 4, 5, 1, 6, 7, 2, 0, 1, 5, 3, 6, 2, 8, 7, 3, 4, 5, 4, 6, 7, 5, 6, 7)
OUTPUTS = tuple(dict(output=0, frames_grad=0, gradients=0))


def split(value):
    high = value.astype(BF16)
    return high, (value - high.astype(F32)).astype(BF16)


def dot(left, right, dims=NN, precision=None):
    return lax.dot_general(
        left, right, (dims, ((), ())), precision=precision, preferred_element_type=F32
    )


def fold(value):
    half = value.shape[1] // 2
    return value[:, :half] + value[:, half:]


def fold_rows(value):
    half = value.shape[0] // 2
    return value[:half] + value[half:]


def tile_sums(value):
    return jnp.sum(value.reshape(-1, 8, value.shape[-1]), axis=0)


def column_sum(tiles):
    return jnp.sum(tiles, axis=0, keepdims=True)


def normal(value):
    bell = jnp.exp(-0.5 * value * value)
    t = 1.0 / (1.0 + 0.2316418882663604 * jnp.abs(value))
    poly = 0.5307027145
    for factor in (-0.7265760135, 0.7107068705, -0.142248368, 0.127414796):
        poly = poly * t + factor
    tail = poly * t * bell
    return jnp.where(value < 0.0, tail, 1.0 - tail), 0.3989422804014327 * bell


def dot_three(left, right, dims=NN):
    left_high, left_low = split(left)
    right_high, right_low = split(right)
    total = dot(left_high, right_high, dims)
    return total + (dot(left_high, right_low, dims) + dot(left_low, right_high, dims))


def group_ones(channels, size):
    rows = lax.broadcasted_iota(jnp.int32, (channels, channels), 0) // size
    columns = lax.broadcasted_iota(jnp.int32, (channels, channels), 1) // size
    return (rows == columns).astype(BF16)


def group_sums(first, second, ones):
    terms = []
    rest = jnp.concatenate([first, second], axis=0)
    for _ in range(3):
        term = rest.astype(BF16)
        terms.append(term)
        rest = rest - term.astype(F32)
    both = dot(jnp.concatenate(terms, axis=0), ones)
    both = both[32:48] + both[16:32] + both[:16]
    return column_sum(both[:8]), column_sum(both[8:])


class LineSwap:

    def __init__(self, line, source, target, inward, across, make):
        far = 3 - line.outer
        self.line = line
        to_inner, to_across = line.device(line.inner), line.device(line.across)
        to_outer = line.device(line.outer)
        here = target(line.here)
        self.to_far = make(source(3 - line.here), inward.at[1], to_inner)
        self.to_second = make(source(3 - line.inner), inward.at[0], to_inner)
        self.to_inner = make(source(line.inner), here, to_inner)
        self.for_far = make(source(far), across.at[0], to_across)
        self.to_across = make(source(line.across), here, to_across)
        self.to_outer = make(source(line.outer), here, to_outer)
        self.pass_far = make(inward.at[1], across.at[1], to_across)
        self.pass_second = make(inward.at[0], target(line.outer), to_across)
        self.pass_across = make(across.at[0], target(line.across), to_outer)
        self.pass_opposite = make(across.at[1], target(far), to_outer)

    def first(self):
        @pl.when(self.line.edge)
        def _():
            for copy in (self.to_far, self.to_second, self.to_inner):
                copy.start()

        @pl.when(self.line.middle)
        def _():
            for copy in (self.for_far, self.to_across, self.to_outer):
                copy.start()

    def second(self):
        @pl.when(self.line.middle)
        def _():
            self.for_far.wait_recv()
            self.pass_across.start()
            self.to_far.wait_recv()
            self.pass_far.start()
            self.to_second.wait_recv()
            self.pass_second.start()

    def third(self):
        @pl.when(self.line.middle)
        def _():
            self.pass_far.wait_recv()
            self.pass_opposite.start()

    def arrive(self):
        @pl.when(self.line.edge)
        def _():
            for copy in (self.to_outer, self.pass_across, self.pass_opposite):
                copy.wait_recv()

        @pl.when(self.line.middle)
        def _():
            for copy in (self.to_inner, self.to_across, self.pass_second):
                copy.wait_recv()

    def sent(self):
        @pl.when(self.line.edge)
        def _():
            for copy in (self.to_far, self.to_second, self.to_inner):
                copy.wait_send()

        @pl.when(self.line.middle)
        def _():
            for copy in (self.for_far, self.to_across, self.to_outer):
                copy.wait_send()
            for copy in (self.pass_far, self.pass_second, self.pass_across, self.pass_opposite):
                copy.wait_send()


class Exchange:

    def __init__(self, place, start, rows, landing, first_sem):
        self.place, self.start, self.rows, self.landing = place, start, rows, landing
        self.sem = first_sem
        self.stage = 0
        self.copies = []
        self.waiting = []
        self.group = place.plane_group
        self.half = rows // 2
        self.base = start + place.core * self.half
        self._finish(self.half)

    def _finish(self, size):
        self.part = size // self.group.count
        self.own = self.base + self.group.here * self.part

    def count(self):
        return 2 * PIECES + 2 * (self.group.count - 1) + 3

    def land_rows(self):
        return self.half + (self.group.count + 1) * self.part

    def _copy(self, source, target, device, only=None):
        place = self.place
        copy = pltpu.make_async_remote_copy(
            src_ref=source,
            dst_ref=target,
            send_sem=place.send.at[self.sem],
            recv_sem=place.recv.at[self.sem],
            device_id=device,
            device_id_type=MESH,
        )
        self.sem += 1
        if only is None:
            copy.start()
            self.waiting.append(copy)
        self.copies.append((copy, only))
        return copy

    def _pieces(self, source, at, target, to, size, device):
        each = size // 8 // PIECES * 8
        for k in range(PIECES):
            here = each if k < PIECES - 1 else size - each * (PIECES - 1)
            self._copy(
                source.at[self._rows(at + k * each, here)],
                target.at[self._rows(to + k * each, here)],
                device,
            )

    def _wait(self):
        for copy in self.waiting:
            copy.wait_recv()
        self.waiting = []

    def _rows(self, at, size):
        return pl.ds(pl.multiple_of(at, 8), size)

    def _swap(self):
        place = self.place
        other = self.start + (1 - place.core) * self.half
        self.land = self.landing
        self.landing += self.half
        self._pieces(place.sums, other, place.landing, self.land, self.half, place.partner)

    def _add_swap(self):
        place = self.place
        block = 64 if self.half % 64 == 0 else 32

        def step(i, carry):
            here = self._rows(self.base + i * block, block)
            there = self._rows(self.land + i * block, block)
            place.sums[here] = place.sums[here] + place.landing[there]
            return carry

        lax.fori_loop(0, self.half // block, step, 0)

    def _scatter(self, group, base, size):
        place = self.place
        self.land = self.landing
        for k in range(1, group.count):
            to = lax.rem(group.here + k, group.count)
            self._copy(
                place.sums.at[self._rows(base + to * size, size)],
                place.landing.at[pl.ds(self.landing, size)],
                group.device(to),
            )
            self.landing += size

    def _total(self, group, own, size, target):
        place = self.place
        block = 16 if size % 16 == 0 else 8

        def step(i, carry):
            here = self._rows(own + i * block, block)
            total = place.sums[here]
            for k in range(group.count - 1):
                there = self._rows(self.land + k * size + i * block, block)
                total = total + place.landing[there]
            target[here] = total
            return carry

        lax.fori_loop(0, size // block, step, 0)

    def _gather(self, group, own, size):
        final = self.place.final
        here = self._rows(own, size)
        for k in range(1, group.count):
            to = lax.rem(group.here + k, group.count)
            self._copy(final.at[here], final.at[here], group.device(to))

    def _steps(self):
        place, group = self.place, self.group
        yield self._swap()
        self._wait()
        self._add_swap()
        yield from self._both()
        self._pieces(place.final, self.base, place.final, self.base, self.half, place.partner)
        yield
        self._wait()
        yield

    def _both(self):
        place, group = self.place, self.group
        self._scatter(group, self.base, self.part)
        yield
        self._wait()
        self._total(group, self.own, self.part, place.sums)
        yield from self._line()
        self._gather(group, self.own, self.part)
        yield
        self._wait()

    def _line(self):
        place, line = self.place, self.place.line
        sums, final, landing = place.sums, place.final, place.landing
        part, own = self.part, self._rows(self.own, self.part)
        inward, across = pl.ds(self.landing, part), pl.ds(self.landing + part, part)
        self.landing += 2 * part
        block = 16 if part % 16 == 0 else 8

        def add(at, target):
            def step(i, carry):
                here = self._rows(self.own + i * block, block)
                target[here] = sums[here] + landing[pl.ds(at + i * block, block)]
                return carry

            lax.fori_loop(0, part // block, step, 0)

        first = self._copy(sums.at[own], landing.at[inward], line.device(line.inner), line.edge)
        second = self._copy(sums.at[own], landing.at[across], line.device(line.across), line.middle)
        third = self._copy(final.at[own], final.at[own], line.device(line.outer), line.middle)
        pl.when(line.edge)(first.start)
        yield

        @pl.when(line.middle)
        def _():
            first.wait_recv()
            add(self.landing - 2 * part, sums)
            second.start()

        yield

        @pl.when(line.middle)
        def _():
            second.wait_recv()
            add(self.landing - part, final)
            third.start()

        yield
        pl.when(line.edge)(third.wait_recv)

    def advance(self):
        if self.stage == 0:
            self.steps = self._steps()
        self.stage += 1
        next(self.steps)

    def done(self):
        return self.stage == 8


class SmallExchange(Exchange):

    def count(self):
        return self.place.cores_group.count + self.place.line.count - 2

    def land_rows(self):
        return self.rows * (self.place.cores_group.count + self.place.line.count)

    def _share(self, group, source):
        place = self.place
        self.land = self.landing
        self.landing += group.count * self.rows
        own = self._rows(self.land + group.here * self.rows, self.rows)
        place.landing[own] = source[...]
        for k in range(1, group.count):
            to = lax.rem(group.here + k, group.count)
            self._copy(source, place.landing.at[own], group.device(to))

    def _sum(self, group):
        total = None
        for k in range(group.count):
            part = self.place.landing[pl.ds(self.land + k * self.rows, self.rows)]
            total = part if total is None else total + part
        return total

    def _steps(self):
        place = self.place
        here = pl.ds(self.start, self.rows)
        self._share(place.line, place.sums.at[here])
        yield
        self._wait()
        place.small[...] = self._sum(place.line)
        self._share(place.cores_group, place.small)
        yield
        self._wait()
        place.final[here] = self._sum(place.cores_group)
        yield

    def done(self):
        return self.stage == 3


def layout_of(shapes):
    starts = {}
    at = 0
    for name in LARGE:
        starts[name] = at
        at += getattr(shapes, name)[0]
    small = at
    begins = SimpleNamespace(**starts)
    late = small + LATE
    tap = shapes.dec_conv2[0] // 3
    part = shapes.dec_conv1[0] // 3
    conv1, up = begins.dec_conv1, begins.up_weight
    edges = (
        (begins.dec_conv2, begins.enc_conv1),
        (conv1, conv1 + part),
        (conv1 + part, conv1 + 2 * part),
        (conv1 + 2 * part, up),
        (up, begins.dec_conv2),
        (begins.enc_conv2, late),
        (begins.enc_conv1, begins.enc_conv1 + 2 * tap),
        (begins.enc_conv1 + 2 * tap, begins.enc_conv2),
        (late, late + LATE_COUNT),
    )
    runs = [(first, last - first) for first, last in edges]
    return starts, small, late + LATE_COUNT, runs


def item_kernel(sizes, scratch_names, *refs):
    line, strip, width, shapes, big_layout = sizes
    begins, small_at, total_rows, runs = big_layout
    starts = SimpleNamespace(**begins)
    inputs = Given(*refs[: len(ARGUMENTS)])
    refs = refs[len(ARGUMENTS) :]
    output_names = OUTPUTS
    outputs = SimpleNamespace(**dict(zip(output_names, refs)))
    scratch = SimpleNamespace(**dict(zip(scratch_names, refs[len(output_names) :])))

    def w_of(name):
        return getattr(scratch, name)

    height = strip * line
    cells = height * width
    c = inputs.lift_weight.shape[1]
    strip_cells = strip * width
    history = inputs.frames.shape[1]

    core = lax.axis_index("section")
    plane = lax.axis_index("batch")
    row = lax.axis_index("rows")
    middle = lax.rem(row + 1, 4) // 2

    def device_at(to):
        return (core, plane, to)

    place = SimpleNamespace(
        core=core,
        partner=(1 - core, plane, row),
        line=SimpleNamespace(
            count=line,
            here=row,
            device=device_at,
            middle=middle == 1,
            edge=middle == 0,
            inner=1 + row // 2,
            across=3 - row,
            outer=3 * (row // 2),
        ),
        plane_group=SimpleNamespace(
            count=4, here=plane, device=lambda to: (core, to, row)
        ),
        cores_group=SimpleNamespace(
            count=8,
            here=core * 4 + plane,
            device=lambda to: (to // 4, lax.rem(to, 4), row),
        ),
        small=scratch.small,
        sums=scratch.sums,
        final=outputs.gradients,
        landing=scratch.landing,
        send=scratch.send,
        recv=scratch.recv,
    )
    local_sem = scratch.local

    frames_in, mask_in, cot = scratch.frames_in, scratch.mask_in, scratch.cot
    here_rows = pl.ds(pl.multiple_of(row * strip_cells, strip_cells), strip_cells)
    frames_from, mask_from, cot_from = scratch.frames_from, scratch.mask_from, scratch.cot_from
    staged = (
        pltpu.make_async_copy(inputs.frames, frames_from, local_sem.at[7]),
        pltpu.make_async_copy(inputs.cell_mask, mask_from, local_sem.at[8]),
        pltpu.make_async_copy(inputs.cotangent, cot_from, local_sem.at[9]),
    )
    for copy in staged:
        copy.start()

    weight_copies = {}
    for k, name in enumerate(LARGE):
        copy = pltpu.make_async_copy(getattr(inputs, name), w_of(name), local_sem.at[k])
        weight_copies[name] = copy
        copy.start()

    barrier = pltpu.get_barrier_semaphore()
    peers = [device_at(lax.rem(row + k, line)) for k in range(1, line)]
    cores_group = place.cores_group
    for k in range(1, 8):
        peers.append(cores_group.device(lax.rem(cores_group.here + k, 8)))
    for device in peers:
        pl.semaphore_signal(barrier, inc=1, device_id=device, device_id_type=MESH)
    pl.semaphore_wait(barrier, len(peers))

    next_sem = 0

    def make(source, target, device):
        nonlocal next_sem
        copy = pltpu.make_async_remote_copy(
            src_ref=source,
            dst_ref=target,
            send_sem=scratch.send.at[next_sem],
            recv_sem=scratch.recv.at[next_sem],
            device_id=device,
            device_id_type=MESH,
        )
        next_sem += 1
        return copy

    def send(source, target, device):
        copy = make(source, target, device)
        copy.start()
        return copy

    def strip_of(ref, to):
        return ref.at[pl.ds(pl.multiple_of(to * strip_cells, strip_cells), strip_cells)]

    frame_copies, output_copies = [], []
    for copy in staged[:2]:
        copy.wait()
    for k in range(1, line):
        to = lax.rem(row + k, line)
        device = device_at(to)
        frame_copies.append(send(frames_from.at[to], frames_in.at[row], device))
        frame_copies.append(send(mask_from.at[to], mask_in.at[row], device))
    staged[2].wait()
    cot_swap = LineSwap(
        place.line,
        lambda to: cot_from.at[to],
        lambda source: strip_of(cot, source),
        scratch.cot_inward,
        scratch.cot_across,
        make,
    )
    cot_swap.first()

    copied = SimpleNamespace(**weight_copies)
    def put_pair(target, block, value):
        high, low = split(value)
        rows = slice(block * c, (block + 1) * c)
        target[rows, 0:c] = high
        target[rows, c : 2 * c] = low

    def stack_conv(source, half, depth, forward, backward):
        for a in range(3):
            for b in range(3):
                at = (3 * a + b) * depth + half * c
                value = source[at : at + c, :]
                turned = value.T
                for places in (HIGH_AT, LOW_AT):
                    put_pair(forward, 6 * a + places[b], value)
                    put_pair(backward, 6 * (2 - a) + places[2 - b], turned)

    copied.enc_conv1.wait()
    stack_conv(scratch.enc_conv1, 0, c, scratch.fe1, scratch.be1)
    copied.enc_conv2.wait()
    stack_conv(scratch.enc_conv2, 0, c, scratch.fe2, scratch.be2)
    copied.reducer_weight.wait()
    for k in range(4):
        value = scratch.reducer_weight[k * c : (k + 1) * c, :]
        turned = value.T
        for block in (k, k + 4):
            put_pair(scratch.f_down, block, value)
        for block in (0, 1):
            put_pair(scratch.b_down.at[k], block, turned)
    copied.up_weight.wait()
    for k in range(4):
        value = scratch.up_weight[k * c : (k + 1) * c, :]
        turned = value.T
        for block in (0, 1):
            put_pair(scratch.f_up.at[k], block, value)
        for block in (k, k + 4):
            put_pair(scratch.b_up, block, turned)
    copied.dec_conv1.wait()
    stack_conv(scratch.dec_conv1, 0, 2 * c, scratch.fd1a, scratch.bd1a)
    stack_conv(scratch.dec_conv1, 1, 2 * c, scratch.fd1b, scratch.bd1b)
    copied.dec_conv2.wait()
    stack_conv(scratch.dec_conv2, 0, c, scratch.fd2, scratch.bd2)
    copied.skip_weight.wait()
    for half in range(2):
        value = scratch.skip_weight[half * c : (half + 1) * c, :]
        turned = value.T
        for block in (half, half + 2):
            put_pair(scratch.f_skip, block, value)
        for block in (0, 1):
            put_pair(scratch.b_skip.at[half], block, turned)

    for buffer in (scratch.xe1, scratch.xe2, scratch.xd1a, scratch.xd1b, scratch.xd2, scratch.xg):
        edge = jnp.zeros((width, 6 * c), BF16)
        buffer[0:width, :] = edge
        buffer[cells + width : cells + 2 * width, :] = edge

    lift = scratch.lift
    lift[...] = jnp.zeros(lift.shape, F32)
    lift[0:history, :] = inputs.lift_weight[...]
    lift[history : history + 1, :] = inputs.lift_bias[...]

    block = 2 * width
    column = lax.rem(lax.broadcasted_iota(jnp.int32, (block, c), 0), width)
    at_first, at_last = column == 0, column == width - 1
    zeros8 = jnp.zeros((8, c), F32)
    ones16 = group_ones(c, c // GROUPS)
    ones32 = group_ones(c, 2 * c // GROUPS)
    count16 = float(cells * (c // GROUPS))
    count32 = float(cells * (2 * c // GROUPS))

    def grid_rows(step, carry=0):
        return lax.fori_loop(0, cells // block, step, carry, unroll=2)

    def row_at(h):
        return pl.ds(pl.multiple_of(h * block, block), block)

    def chunk_at(i):
        return pl.ds(pl.multiple_of(i * CHUNK, CHUNK), CHUNK)

    def put_row(target, h, value):
        rows = pl.ds(pl.multiple_of(h * block + width, width), block)
        left = jnp.where(at_first, 0.0, pltpu.roll(value, 1, 0))
        right = jnp.where(at_last, 0.0, pltpu.roll(value, block - 1, 0))
        for b, piece in enumerate((left, value, right)):
            high, low = split(piece)
            target[rows, HIGH_AT[b] * c : (HIGH_AT[b] + 1) * c] = high
            target[rows, LOW_AT[b] * c : (LOW_AT[b] + 1) * c] = low

    def put_turned(target, columns, value, first=0, second=1):
        high, low = split(value.T)
        target[first * c : (first + 1) * c, columns] = high
        target[second * c : (second + 1) * c, columns] = low

    def conv_chunk(pairs, i):
        total = None
        for data, weight in pairs:
            taps = []
            for a in range(3):
                rows = pl.ds(pl.multiple_of(i * CHUNK + a * width, width), CHUNK)
                taps.append(data[rows, :])
            part = dot(jnp.concatenate(taps, axis=1), weight[...])
            total = part if total is None else total + part
        return total

    def norm_of(first, second, ones, count):
        one, two = group_sums(first, second, ones)
        mean = one / count
        return mean, lax.rsqrt(two / count - mean * mean + EPS)

    def activate(source, target, turned, slope, scale, shift):
        def step(h, carry):
            value = source[row_at(h), :] * scale + shift
            below, density = normal(value)
            slope[row_at(h), :] = below + value * density
            value = value * below
            put_row(target, h, value)
            put_turned(turned, row_at(h), value)
            return carry

        grid_rows(step)

    def conv_norm(pairs, target):
        def step(i, carry):
            value = fold(conv_chunk(pairs, i))
            target[chunk_at(i), :] = value
            return carry[0] + tile_sums(value), carry[1] + tile_sums(value * value)

        return lax.fori_loop(0, cells // CHUNK, step, (zeros8, zeros8))

    def sums_of(source):
        def step(h, carry):
            value = source[row_at(h), :]
            return carry[0] + tile_sums(value), carry[1] + tile_sums(value * value)

        return grid_rows(step, (zeros8, zeros8))

    step_here = jnp.full((1, c), inputs.step_index[row], jnp.int32)

    def condition(table):
        total = jnp.zeros((1, 2 * c), F32)
        chosen = jnp.concatenate([step_here, step_here], axis=1)
        for s in range(table.shape[0]):
            total = total + jnp.where(chosen == s, table[s : s + 1, :], 0.0)
        return total[:, :c], total[:, c:]

    frames_in[row] = frames_from[row]
    mask_in[row] = mask_from[row]
    for copy in frame_copies:
        copy.wait_recv()
    fields = scratch.fields
    fields[...] = jnp.zeros(fields.shape, F32)
    frame_of = lax.broadcasted_iota(jnp.int32, (history, width), 0) // FIELDS
    keep = (frame_of >= HIST - inputs.counts[row]).astype(F32)
    masks = []
    for source in range(line):
        for k in range(strip):
            columns = slice((source * strip + k) * width, (source * strip + k + 1) * width)
            mask = mask_in[source, k : k + 1, :].astype(F32)
            masks.append(mask)
            fields[0:history, columns] = frames_in[source, :, k, :] * keep * mask
            fields[history : history + 1, columns] = mask
    lifted = scratch.lifted
    lifted[...] = dot_three(fields[...], lift[...], TN)

    enc_scale, enc_shift = condition(inputs.enc_step_table)
    dec_scale, dec_shift = condition(inputs.dec_step_table)

    mean_e1, inv_e1 = norm_of(*sums_of(lifted), ones16, count16)
    gain_e1, bias_e1 = inputs.enc_norm1_gain[...], inputs.enc_norm1_bias[...]
    a_e1 = inv_e1 * gain_e1
    activate(lifted, scratch.xe1, scratch.te1, scratch.slope_e1, a_e1, bias_e1 - mean_e1 * a_e1)
    middle_e = scratch.middle_e
    mean_e2, inv_e2 = norm_of(
        *conv_norm([(scratch.xe1, scratch.fe1)], middle_e), ones16, count16
    )
    gain_e2, bias_e2 = inputs.enc_norm2_gain[...], inputs.enc_norm2_bias[...]
    a_e2 = inv_e2 * gain_e2
    activate(
        middle_e,
        scratch.xe2,
        scratch.te2,
        scratch.slope_e2,
        a_e2 * (1.0 + enc_scale),
        (bias_e2 - mean_e2 * a_e2) * (1.0 + enc_scale) + enc_shift,
    )
    cot_swap.second()
    encoded = scratch.encoded
    conv2_bias = inputs.enc_conv2_bias[...]
    joined = scratch.joined

    def encode(i, carry):
        value = fold(conv_chunk([(scratch.xe2, scratch.fe2)], i))
        value = value + conv2_bias + lifted[chunk_at(i), :]
        encoded[chunk_at(i), :] = value
        high, low = split(value)
        joined[chunk_at(i), c : 2 * c] = high
        joined[chunk_at(i), 3 * c : 4 * c] = low
        put_turned(scratch.turned, chunk_at(i), value, 1, 3)
        return carry[0] + tile_sums(value), carry[1] + tile_sums(value * value)

    sums_enc = lax.fori_loop(0, cells // CHUNK, encode, (zeros8, zeros8))

    half_cells, quarter = cells // 2, cells // 4

    def pick(source):
        pieces = []
        for b in range(2):
            value = source[pl.ds(b, half_cells, stride=2), :]
            value = value.reshape(height // 2, 2, width // 2, c)
            pieces.append([value[:, a].reshape(quarter, c) for a in range(2)])
        return [pieces[b][a] for a in range(2) for b in range(2)]

    def place_cells(target, pieces):
        for b in range(2):
            both = [pieces[2 * a + b].reshape(height // 2, 1, width // 2, c) for a in range(2)]
            value = jnp.concatenate(both, axis=1).reshape(half_cells, c)
            target[pl.ds(b, half_cells, stride=2), :] = value

    x_down = scratch.x_down
    for k, piece in enumerate(pick(encoded)):
        high, low = split(piece)
        x_down[:, k * c : (k + 1) * c] = high
        x_down[:, (k + 4) * c : (k + 5) * c] = low
    lowered = fold(dot(x_down[...], scratch.f_down[...])) + inputs.reducer_bias[...]
    x_up = scratch.x_up
    high, low = split(lowered)
    x_up[:, 0:c] = high
    x_up[:, c : 2 * c] = low
    raised = scratch.raised
    up_bias = inputs.up_bias[...]
    place_cells(
        raised, [fold(dot(x_up[...], scratch.f_up[k])) + up_bias for k in range(4)]
    )

    def raise_row(h, carry):
        value = raised[row_at(h), :]
        high, low = split(value)
        joined[row_at(h), 0:c] = high
        joined[row_at(h), 2 * c : 3 * c] = low
        put_turned(scratch.turned, row_at(h), value, 0, 2)
        return carry[0] + tile_sums(value), carry[1] + tile_sums(value * value)

    sums_raised = grid_rows(raise_row, (zeros8, zeros8))

    halves = []
    for half, (source, sums) in enumerate(((raised, sums_raised), (encoded, sums_enc))):
        mean, inv = norm_of(*sums, ones32, count32)
        gain = inputs.dec_norm1_gain[half : half + 1, :]
        bias = inputs.dec_norm1_bias[half : half + 1, :]
        scale = inv * gain
        activate(
            source,
            (scratch.xd1a, scratch.xd1b)[half],
            scratch.td1.at[2 * c * half : 2 * c * (half + 1)],
            (scratch.slope_d1a, scratch.slope_d1b)[half],
            scale,
            bias - mean * scale,
        )
        halves.append((source, mean, inv, gain))
    middle_d = scratch.middle_d
    pairs = [(scratch.xd1a, scratch.fd1a), (scratch.xd1b, scratch.fd1b)]
    mean_d2, inv_d2 = norm_of(*conv_norm(pairs, middle_d), ones16, count16)
    cot_swap.third()
    gain_d2, bias_d2 = inputs.dec_norm2_gain[...], inputs.dec_norm2_bias[...]
    a_d2 = inv_d2 * gain_d2
    activate(
        middle_d,
        scratch.xd2,
        scratch.td2,
        scratch.slope_d2,
        a_d2 * (1.0 + dec_scale),
        (bias_d2 - mean_d2 * a_d2) * (1.0 + dec_scale) + dec_shift,
    )
    result = scratch.result
    last_bias = inputs.dec_conv2_bias[...] + inputs.skip_bias[...]

    def decode(i, carry):
        value = conv_chunk([(scratch.xd2, scratch.fd2)], i)
        value = value + dot(joined[chunk_at(i), :], scratch.f_skip[...])
        result[chunk_at(i), :] = fold(value) + last_bias
        return carry

    lax.fori_loop(0, cells // CHUNK, decode, 0)
    output_here, frames_here = outputs.output, outputs.frames_grad
    output_here[row] = result[here_rows]
    output_swap = LineSwap(
        place.line,
        lambda to: strip_of(result, to),
        lambda source: output_here.at[source],
        scratch.output_inward,
        scratch.output_across,
        make,
    )
    output_swap.first()

    exchanges = []
    waiting_runs = list(runs)
    landing_at = 0
    sem_at = 3 * (line - 1) + 20
    sums = scratch.sums

    def begin():
        nonlocal landing_at, sem_at
        start, rows = waiting_runs.pop(0)
        kind = Exchange if waiting_runs else SmallExchange
        exchange = kind(place, start, rows, landing_at, sem_at)
        landing_at += exchange.land_rows()
        sem_at += exchange.count()
        exchanges.append(exchange)
        exchange.advance()

    def advance(k):
        exchange = exchanges[k]
        exchange.advance()

    due = list(DUE)

    def point():
        for k in due.pop(0):
            advance(k)

    def small_row(k, value):
        sums[small_at + k : small_at + k + 1, :] = value

    def spread_grad(source):
        def step(h, carry):
            value = source[row_at(h), :]
            put_row(scratch.xg, h, value)
            return carry + tile_sums(value)

        return grid_rows(step, zeros8)

    def weight_grad(turned, at, depth, a):
        rows = pl.ds((2 - a) * width, cells)
        both = dot(turned[...], scratch.xg[rows, :])
        for half in range(depth // c):
            part = fold_rows(both[2 * c * half : 2 * c * (half + 1)])
            for b in range(3):
                high, low = HIGH_AT[2 - b] * c, LOW_AT[2 - b] * c
                to = at + (3 * a + b) * depth + half * c
                sums[to : to + c, :] = part[:, high : high + c] + part[:, low : low + c]

    def back_conv(weight, slope, target, source, mean, inv):
        carry = (zeros8, zeros8)
        for i in range(cells // CHUNK):
            value = fold(conv_chunk([(scratch.xg, weight)], i)) * slope[chunk_at(i), :]
            target[chunk_at(i), :] = value
            normed = (source[chunk_at(i), :] - mean) * inv
            carry = (carry[0] + tile_sums(value), carry[1] + tile_sums(value * normed))
            if i % (cells // CHUNK // 2) == cells // CHUNK // 2 - 1:
                point()
        return carry

    def norm_grad(sums_in, scale, ones, count):
        one, two = group_sums(sums_in[0] * scale, sums_in[1] * scale, ones)
        return one / count, two / count

    cot[here_rows] = cot_from[row]
    cot_swap.arrive()
    total_cot = column_sum(spread_grad(cot))
    for a in range(3):
        weight_grad(scratch.td2, starts.dec_conv2, c, a)
    part = fold(dot(scratch.turned[...], scratch.xg[width : cells + width, 2 * c : 4 * c]))
    sums[starts.skip_weight : starts.skip_weight + 2 * c, :] = fold_rows(part)
    small_row(3, total_cot)
    begin()

    grad = scratch.grad
    sums_d2 = back_conv(scratch.bd2, scratch.slope_d2, grad, middle_d, mean_d2, inv_d2)
    side_grads = (scratch.grad_a, scratch.grad_b)
    for half in range(2):

        def skip_back(i, carry, half=half):
            rows = pl.ds(pl.multiple_of(i * CHUNK + width, width), CHUNK)
            value = dot(scratch.xg[rows, 2 * c : 4 * c], scratch.b_skip[half])
            side_grads[half][chunk_at(i), :] = fold(value)
            return carry

        lax.fori_loop(0, cells // CHUNK, skip_back, 0)
    point()

    def table_rows(k, sums_in, gain, bias, one_plus):
        plain, times = column_sum(sums_in[0]), column_sum(sums_in[1])
        for s in range(inputs.enc_step_table.shape[0]):
            small_row(k + 2 * s, jnp.where(step_here == s, gain * times + bias * plain, 0.0))
            small_row(k + 2 * s + 1, jnp.where(step_here == s, plain, 0.0))
        return one_plus * times, one_plus * plain

    def middle_grad(source, mean, inv, scale, sums_in):
        zero, slope = norm_grad(sums_in, scale, ones16, count16)

        def step(h, carry):
            normed = (source[row_at(h), :] - mean) * inv
            value = inv * (grad[row_at(h), :] * scale - zero - normed * slope)
            put_row(scratch.xg, h, value)
            return carry

        grid_rows(step)

    gain_row, bias_row = table_rows(16, sums_d2, gain_d2, bias_d2, 1.0 + dec_scale)
    small_row(8, gain_row)
    small_row(9, bias_row)
    middle_grad(middle_d, mean_d2, inv_d2, gain_d2 * (1.0 + dec_scale), sums_d2)
    point()
    output_swap.second()
    for a in range(3):
        weight_grad(scratch.td1, starts.dec_conv1, 2 * c, a)
        point()
        begin()

    for half, (source, mean, inv, gain) in enumerate(halves):
        sums_in = back_conv(
            (scratch.bd1a, scratch.bd1b)[half],
            (scratch.slope_d1a, scratch.slope_d1b)[half],
            grad,
            source,
            mean,
            inv,
        )
        small_row(4 + half, column_sum(sums_in[1]))
        small_row(6 + half, column_sum(sums_in[0]))
        zero, slope = norm_grad(sums_in, gain, ones32, count32)
        target = side_grads[half]

        def input_grad(h, carry):
            normed = (source[row_at(h), :] - mean) * inv
            value = inv * (grad[row_at(h), :] * gain - zero - normed * slope)
            value = target[row_at(h), :] + value
            target[row_at(h), :] = value
            return carry + tile_sums(value)

        total = grid_rows(input_grad, zeros8)
        if half == 0:
            small_row(2, column_sum(total))
        point()

    output_swap.third()
    grad_raised, grad_encoded = side_grads
    x_grad_up = scratch.x_grad_up
    for k, piece in enumerate(pick(grad_raised)):
        high, low = split(piece)
        x_grad_up[:, k * c : (k + 1) * c] = high
        x_grad_up[:, (k + 4) * c : (k + 5) * c] = low
    grad_lowered = fold(dot(x_grad_up[...], scratch.b_up[...]))
    small_row(1, jnp.sum(grad_lowered, axis=0, keepdims=True))
    x_grad_low = scratch.x_grad_low
    high, low = split(grad_lowered)
    x_grad_low[:, 0:c] = high
    x_grad_low[:, c : 2 * c] = low
    point()
    part = fold(fold_rows(dot(x_up[...], x_grad_up[...], TN)))
    for k in range(4):
        at = starts.up_weight + k * c
        sums[at : at + c, :] = part[:, k * c : (k + 1) * c]
    part = fold_rows(fold(dot(x_down[...], x_grad_low[...], TN)))
    sums[starts.reducer_weight : starts.reducer_weight + 4 * c, :] = part
    point()
    begin()
    place_cells(
        grad, [fold(dot(x_grad_low[...], scratch.b_down[k])) for k in range(4)]
    )

    def join_row(h, carry):
        value = grad_encoded[row_at(h), :] + grad[row_at(h), :]
        grad_encoded[row_at(h), :] = value
        put_row(scratch.xg, h, value)
        return carry + tile_sums(value)

    small_row(0, column_sum(grid_rows(join_row, zeros8)))
    for k in range(10, 16):
        small_row(k, jnp.zeros((1, c), F32))
    sums[small_at + 24 : small_at + LATE, :] = jnp.zeros((LATE - 24, c), F32)
    point()
    for a in range(3):
        weight_grad(scratch.te2, starts.enc_conv2, c, a)
        point()
    begin()
    sums_e2 = back_conv(scratch.be2, scratch.slope_e2, grad, middle_e, mean_e2, inv_e2)
    gain_row, bias_row = table_rows(LATE + 24, sums_e2, gain_e2, bias_e2, 1.0 + enc_scale)
    small_row(LATE + 18, gain_row)
    small_row(LATE + 19, bias_row)
    middle_grad(middle_e, mean_e2, inv_e2, gain_e2 * (1.0 + enc_scale), sums_e2)
    point()
    for a in range(3):
        weight_grad(scratch.te1, starts.enc_conv1, c, a)
        point()
        if a:
            begin()
    sums_e1 = back_conv(scratch.be1, scratch.slope_e1, grad, lifted, mean_e1, inv_e1)
    small_row(LATE + 16, column_sum(sums_e1[1]))
    small_row(LATE + 17, column_sum(sums_e1[0]))
    zero, slope = norm_grad(sums_e1, gain_e1, ones16, count16)

    def lifted_grad(h, carry):
        normed = (lifted[row_at(h), :] - mean_e1) * inv_e1
        value = inv_e1 * (grad[row_at(h), :] * gain_e1 - zero - normed * slope)
        grad[row_at(h), :] = grad_encoded[row_at(h), :] + value
        return carry

    grid_rows(lifted_grad)
    point()

    late_at = small_at + LATE
    sums[late_at : late_at + 16, :] = dot_three(fields[...], grad[...])
    sums[late_at + 20 : late_at + 24, :] = jnp.zeros((4, c), F32)
    point()
    begin()
    back = dot_three(lift[...], grad[...], NT)
    frames_out = scratch.frames_out
    for source in range(line):
        for k in range(strip):
            h = source * strip + k
            value = back[0:history, h * width : (h + 1) * width]
            frames_out[source, :, k, :] = value * keep * masks[h]
    frames_here[row] = frames_out[row]
    for k in range(1, line):
        to = lax.rem(row + k, line)
        output_copies.append(
            send(frames_out.at[to], frames_here.at[row], device_at(to))
        )

    output_swap.arrive()
    for k in REST:
        advance(k)
    assert not due and all(exchange.done() for exchange in exchanges)

    for copy in output_copies:
        copy.wait_recv()
    for copy in frame_copies + output_copies:
        copy.wait_send()
    cot_swap.sent()
    output_swap.sent()
    for exchange in exchanges:
        for copy, only in exchange.copies:
            if only is None:
                copy.wait_send()
            else:
                pl.when(only)(copy.wait_send)


def write_kernel(layout, *refs):
    shapes, starts, small_at = layout
    output, frames_grad, gradients_here = refs[:3]
    outputs = refs[3:-1]
    sem = refs[-1]
    c = gradients_here.shape[1]
    leaving = []

    def leave(source, target):
        leaving.append(pltpu.make_async_copy(source, target, sem.at[len(leaving)]))
        leaving[-1].start()

    for k, name in enumerate(LARGE):
        rows = pl.ds(starts[name], shapes[name][0])
        leave(gradients_here.at[rows], outputs[2 + k])
    for target, (k, rows) in zip(outputs[2 + len(LARGE) :], SMALL_ROWS.values()):
        at = small_at + k
        if rows == 8:
            for s in range(target.shape[0]):
                target[s : s + 1, 0:c] = gradients_here[at + 2 * s : at + 2 * s + 1, :]
                target[s : s + 1, c : 2 * c] = gradients_here[at + 2 * s + 1 : at + 2 * s + 2, :]
        else:
            target[...] = gradients_here[at : at + rows, :]
    leave(output, outputs[0])
    leave(frames_grad, outputs[1])
    for copy in leaving:
        copy.wait()


def whole_items(shape, *arguments):
    line = shape["rows"]
    whole = Given(*arguments)
    given = whole._asdict()
    frames, cotangent = whole.frames, whole.cotangent
    items, history, strip, width = frames.shape
    c = cotangent.shape[-1]
    cells = strip * line * width
    flat = {}
    for name, value in given.items():
        if value is cotangent:
            value = value.reshape(items, strip * width, c)
        elif name in LARGE:
            value = value.reshape(-1, c)
        elif value.ndim == 1 and name not in IN_SMEM:
            value = value.reshape(-1, c)
        flat[name] = value
    shapes = {name: flat[name].shape for name in LARGE}
    big_layout = layout_of(SimpleNamespace(**shapes))
    starts, small_at, total_rows, runs = big_layout
    copies = 20 + 3 * (line - 1) + len(runs) * (6 + 2 * PIECES + 2 * (line - 1)) + 6
    landing = sum(rows // 2 + 5 * rows // 8 for _, rows in runs) + LATE_COUNT * (8 + line)
    shifted = pltpu.VMEM((cells + 2 * width, 6 * c), BF16)
    forward = pltpu.VMEM((18 * c, 2 * c), BF16)
    backward = forward
    field = pltpu.VMEM((cells, c), F32)
    flipped_field = pltpu.VMEM((2 * c, cells), BF16)
    quarter = cells // 4
    scratch = dict(
        small=pltpu.VMEM((LATE_COUNT, c), F32),
        send=pltpu.SemaphoreType.DMA((copies,)),
        recv=pltpu.SemaphoreType.DMA((copies,)),
        local=pltpu.SemaphoreType.DMA((12 + len(runs),)),
        sums=pltpu.VMEM((total_rows, c), F32),
        landing=pltpu.VMEM((landing, c), F32),
        frames_in=pltpu.VMEM((line, history, strip, width), F32),
        mask_in=pltpu.VMEM((line, strip, width), jnp.int32),
        frames_out=pltpu.VMEM((line, history, strip, width), F32),
        frames_from=pltpu.VMEM((line, history, strip, width), F32),
        mask_from=pltpu.VMEM((line, strip, width), jnp.int32),
        cot_from=pltpu.VMEM((items, strip * width, c), F32),
        cot_inward=pltpu.VMEM((2, strip * width, c), F32),
        cot_across=pltpu.VMEM((2, strip * width, c), F32),
        output_inward=pltpu.VMEM((2, strip * width, c), F32),
        output_across=pltpu.VMEM((2, strip * width, c), F32),
        fields=pltpu.VMEM((16, cells), F32),
        lift=pltpu.VMEM((16, c), F32),
        joined=pltpu.VMEM((cells, 4 * c), BF16),
        x_down=pltpu.VMEM((quarter, 8 * c), BF16),
        x_grad_up=pltpu.VMEM((quarter, 8 * c), BF16),
        x_up=pltpu.VMEM((quarter, 2 * c), BF16),
        x_grad_low=pltpu.VMEM((quarter, 2 * c), BF16),
        f_down=pltpu.VMEM((8 * c, 2 * c), BF16),
        b_down=pltpu.VMEM((4, 2 * c, 2 * c), BF16),
        f_up=pltpu.VMEM((4, 2 * c, 2 * c), BF16),
        b_up=pltpu.VMEM((8 * c, 2 * c), BF16),
        f_skip=pltpu.VMEM((4 * c, 2 * c), BF16),
        b_skip=pltpu.VMEM((2, 2 * c, 2 * c), BF16),
        xe1=shifted,
        xe2=shifted,
        xd1a=shifted,
        xd1b=shifted,
        xd2=shifted,
        xg=shifted,
        te1=flipped_field,
        te2=flipped_field,
        td1=pltpu.VMEM((4 * c, cells), BF16),
        td2=flipped_field,
        turned=pltpu.VMEM((4 * c, cells), BF16),
        fe1=forward,
        fe2=forward,
        fd1a=forward,
        fd1b=forward,
        fd2=forward,
        be1=backward,
        be2=backward,
        bd1a=backward,
        bd1b=backward,
        bd2=backward,
        slope_e1=field,
        slope_e2=field,
        slope_d1a=field,
        slope_d1b=field,
        slope_d2=field,
        lifted=field,
        middle_e=field,
        encoded=field,
        raised=field,
        middle_d=field,
        result=field,
        cot=field,
        grad=field,
        grad_a=field,
        grad_b=field,
    )
    scratch.update({name: pltpu.VMEM(shapes[name], F32) for name in LARGE})

    in_hbm = pl.BlockSpec(memory_space=pl.ANY)
    in_vmem = pl.BlockSpec(memory_space=pltpu.VMEM)
    in_smem = pl.BlockSpec(memory_space=pltpu.SMEM)
    in_specs = [
        in_hbm if name in IN_HBM else in_smem if name in IN_SMEM else in_vmem
        for name in ARGUMENTS
    ]
    out_shape = [
        pltpu.VMEM((items, strip * width, c), F32),
        pltpu.VMEM(frames.shape, F32),
        pltpu.VMEM((total_rows, c), F32),
    ]
    out_specs = [in_vmem] * 3
    results = pl.pallas_call(
        functools.partial(
            item_kernel,
            (line, strip, width, shapes, big_layout),
            tuple(scratch),
        ),
        out_shape=out_shape,
        in_specs=in_specs,
        out_specs=out_specs,
        scratch_shapes=list(scratch.values()),
        compiler_params=pltpu.CompilerParams(
            collective_id=0, has_side_effects=True, vmem_limit_bytes=56 * 1024 * 1024
        ),
    )(*[flat[name] for name in ARGUMENTS])
    names = LARGE + tuple(SMALL_ROWS)
    written = pl.pallas_call(
        functools.partial(write_kernel, (shapes, starts, small_at)),
        out_shape=[
            jax.ShapeDtypeStruct((items, strip * width, c), F32),
            jax.ShapeDtypeStruct(frames.shape, F32),
        ]
        + [jax.ShapeDtypeStruct(flat[name].shape, F32) for name in names],
        in_specs=[in_vmem] * 3,
        out_specs=[in_hbm] * (2 + len(LARGE)) + [in_vmem] * len(SMALL_ROWS),
        scratch_shapes=[pltpu.SemaphoreType.DMA((2 + len(LARGE),))],
        compiler_params=pltpu.CompilerParams(vmem_limit_bytes=16 * 1024 * 1024),
    )(*results)
    grads = dict(zip(names, written[2:]))
    ordered = [name for name in ARGUMENTS if name in grads]
    return (written[0].reshape(cotangent.shape), written[1]) + tuple(
        grads[name].reshape(given[name].shape) for name in ordered
    )


def body(shape, *arguments):
    items, _, strip, width = arguments[0].shape
    line = shape["rows"]
    whole = (
        shape["section"] == 2
        and shape["batch"] == 4
        and items == line == 4
        and arguments[-1].shape[-1] == 128
        and (strip * line * width) % CHUNK == 0
    )
    return whole_items(shape, *arguments) if whole else strips_body(*arguments)


def solution(mesh):
    in_specs = (
        P(("section", "batch"), None, "rows", None),
        P(("section", "batch")),
        P(("section", "batch"), "rows", None),
        P(("section", "batch")),
        P(),
        P(),
        P(),
        P(),
        P(),
        P(),
        P(),
        P(),
        P(),
        P(),
        P(),
        P(),
        P(),
        P(),
        P(),
        P(),
        P(),
        P(),
        P(),
        P(),
        P(),
        P(),
        P(),
        P(),
        P(("section", "batch"), "rows", None, None),
    )
    out_specs = (
        P(("section", "batch"), "rows", None, None),
        P(("section", "batch"), None, "rows", None),
        P(),
        P(),
        P(),
        P(),
        P(),
        P(),
        P(),
        P(),
        P(),
        P(),
        P(),
        P(),
        P(),
        P(),
        P(),
        P(),
        P(),
        P(),
        P(),
        P(),
        P(),
        P(),
        P(),
        P(),
    )
    return jax.shard_map(functools.partial(body, mesh.shape), mesh=mesh, in_specs=in_specs, out_specs=out_specs, check_vma=False)
```

profile of v0, /device:TPU:1, one launch (start us, length us, event | category | flops | bytes accessed | tf_op | source)
XLA Modules:
  0.0 90.3 jit_solution(4697611406609907694)
XLA Ops:
  0.7 86.7 %shard_map.476 = (f32[4,256,128]{2,1,0:T(8,128)S(1)}, f32[4,12,4,64]{3,2,1,0:T(4,128)S(1)}, f32[7136,128]{1,0:T(8,128)S(1)}) custom-call(f32[4,12,4,64]{3,2,1,0:T(4,128)} %refs_0_.1, s32[4]{0:T(128)} %refs_1_.1, s32[4,4,64]{2,1,0:T(4,128)} %refs_2_.1, s32[4]{0:T(128)} %refs_3_.1, f32[12,128]{1,0:T(8,128)} %refs_4_.1, f32[1,128]{1,0:T(1,128)} %bitcast.51, ...), custom_call_target="tpu_custom_call" | custom-call | tf_op jit(solution)/shard_map/pallas_call | solution.py:1666
  87.4 2.8 %shard_map.477 = (f32[4,256,128]{2,1,0:T(8,128)}, f32[4,12,4,64]{3,2,1,0:T(4,128)}, f32[2304,128]{1,0:T(8,128)}, f32[512,128]{1,0:T(8,128)}, f32[512,128]{1,0:T(...) custom-call(f32[4,256,128]{2,1,0:T(8,128)S(1)} %get-tuple-element.55, ...), custom_call_target="tpu_custom_call" | custom-call | tf_op jit(solution)/shard_map/pallas_call | solution.py:1681
where the time goes:
time: 90.5 us; the launch traced here: 90.3 us
  Pallas kernels  89.5 us (99%)
    pallas_call x1, Pallas kernels, whole_items(): pl.pallas_call(functools.partial(item_kernel, (line, strip, width, shapes...  86.7 us
    pallas_call x1, Pallas kernels, whole_items(): pl.pallas_call(functools.partial(write_kernel, (shapes, starts, small_at)...  2.75 us

commit v1 on v0

--- a/solution.py
+++ b/solution.py
@@ -468,8 +468,8 @@
 LATE_COUNT = 32
 PIECES = 1
 SMALL_COUNT = LATE + LATE_COUNT
-DUE = ((), (), (), (), (), (0,), (), (1,), (), (), (2,), (3, 0), (), (), (1,), (), (), (2,), (0,), (1, 4, 3), (2,), (), (), (5, 0), (1, 3), (4, 2), (), (6,), (7, 3, 0, 5, 4, 1, 2))
-REST = (6, 3, 7, 4, 5, 6, 8, 7, 0, 4, 5, 1, 6, 7, 2, 0, 1, 5, 3, 6, 2, 8, 7, 3, 4, 5, 4, 6, 7, 5, 6, 7)
+DUE = ((), (), (), (), (0,), (), (), (), (), (1,), (2, 0), (3,), (), (), (1,), (), (0, 2), (), (), (1, 3), (4, 2), (0,), (1, 3), (5,), (2,), (), (4, 0, 3), (1, 6, 2, 7, 5, 4), (), (3,))
+REST = (0, 4, 5, 1, 8, 6, 0, 4, 5, 1, 2, 7, 6, 3, 2, 5, 7, 8, 6, 3, 4, 7, 6, 5, 7, 4, 6, 5, 7, 6, 7)
 OUTPUTS = tuple(dict(output=0, frames_grad=0, gradients=0))
 
 
@@ -991,20 +991,25 @@
         target[rows, 0:c] = high
         target[rows, c : 2 * c] = low
 
-    def stack_conv(source, half, depth, forward, backward):
+    def stack_conv(source, half, depth, forward):
         for a in range(3):
             for b in range(3):
                 at = (3 * a + b) * depth + half * c
-                value = source[at : at + c, :]
-                turned = value.T
                 for places in (HIGH_AT, LOW_AT):
-                    put_pair(forward, 6 * a + places[b], value)
+                    put_pair(forward, 6 * a + places[b], source[at : at + c, :])
+
+    def stack_turned(source, half, depth, backward):
+        for a in range(3):
+            for b in range(3):
+                at = (3 * a + b) * depth + half * c
+                turned = source[at : at + c, :].T
+                for places in (HIGH_AT, LOW_AT):
                     put_pair(backward, 6 * (2 - a) + places[2 - b], turned)
 
     copied.enc_conv1.wait()
-    stack_conv(scratch.enc_conv1, 0, c, scratch.fe1, scratch.be1)
+    stack_conv(scratch.enc_conv1, 0, c, scratch.fe1)
     copied.enc_conv2.wait()
-    stack_conv(scratch.enc_conv2, 0, c, scratch.fe2, scratch.be2)
+    stack_conv(scratch.enc_conv2, 0, c, scratch.fe2)
     copied.reducer_weight.wait()
     for k in range(4):
         value = scratch.reducer_weight[k * c : (k + 1) * c, :]
@@ -1022,10 +1027,10 @@
         for block in (k, k + 4):
             put_pair(scratch.b_up, block, turned)
     copied.dec_conv1.wait()
-    stack_conv(scratch.dec_conv1, 0, 2 * c, scratch.fd1a, scratch.bd1a)
-    stack_conv(scratch.dec_conv1, 1, 2 * c, scratch.fd1b, scratch.bd1b)
+    stack_conv(scratch.dec_conv1, 0, 2 * c, scratch.fd1a)
+    stack_conv(scratch.dec_conv1, 1, 2 * c, scratch.fd1b)
     copied.dec_conv2.wait()
-    stack_conv(scratch.dec_conv2, 0, c, scratch.fd2, scratch.bd2)
+    stack_conv(scratch.dec_conv2, 0, c, scratch.fd2)
     copied.skip_weight.wait()
     for half in range(2):
         value = scratch.skip_weight[half * c : (half + 1) * c, :]
@@ -1257,6 +1262,78 @@
         a_d2 * (1.0 + dec_scale),
         (bias_d2 - mean_d2 * a_d2) * (1.0 + dec_scale) + dec_shift,
     )
+    exchanges = []
+    waiting_runs = list(runs)
+    landing_at = 0
+    sem_at = 3 * (line - 1) + 20
+    sums = scratch.sums
+
+    def begin():
+        nonlocal landing_at, sem_at
+        start, rows = waiting_runs.pop(0)
+        kind = Exchange if waiting_runs else SmallExchange
+        exchange = kind(place, start, rows, landing_at, sem_at)
+        landing_at += exchange.land_rows()
+        sem_at += exchange.count()
+        exchanges.append(exchange)
+        exchange.advance()
+
+    def advance(k):
+        exchange = exchanges[k]
+        exchange.advance()
+
+    due = list(DUE)
+
+    def point():
+        for k in due.pop(0):
+            advance(k)
+
+    def small_row(k, value):
+        sums[small_at + k : small_at + k + 1, :] = value
+
+    def spread_grad(source):
+        def step(h, carry):
+            value = source[row_at(h), :]
+            put_row(scratch.xg, h, value)
+            return carry + tile_sums(value)
+
+        return grid_rows(step, zeros8)
+
+    def weight_grad(turned, at, depth, a):
+        rows = pl.ds((2 - a) * width, cells)
+        both = dot(turned[...], scratch.xg[rows, :])
+        for half in range(depth // c):
+            part = fold_rows(both[2 * c * half : 2 * c * (half + 1)])
+            for b in range(3):
+                high, low = HIGH_AT[2 - b] * c, LOW_AT[2 - b] * c
+                to = at + (3 * a + b) * depth + half * c
+                sums[to : to + c, :] = part[:, high : high + c] + part[:, low : low + c]
+
+    def back_conv(weight, slope, target, source, mean, inv):
+        carry = (zeros8, zeros8)
+        for i in range(cells // CHUNK):
+            value = fold(conv_chunk([(scratch.xg, weight)], i)) * slope[chunk_at(i), :]
+            target[chunk_at(i), :] = value
+            normed = (source[chunk_at(i), :] - mean) * inv
+            carry = (carry[0] + tile_sums(value), carry[1] + tile_sums(value * normed))
+            if i % (cells // CHUNK // 2) == cells // CHUNK // 2 - 1:
+                point()
+        return carry
+
+    def norm_grad(sums_in, scale, ones, count):
+        one, two = group_sums(sums_in[0] * scale, sums_in[1] * scale, ones)
+        return one / count, two / count
+
+    cot[here_rows] = cot_from[row]
+    cot_swap.arrive()
+    total_cot = column_sum(spread_grad(cot))
+    for a in range(3):
+        weight_grad(scratch.td2, starts.dec_conv2, c, a)
+    part = fold(dot(scratch.turned[...], scratch.xg[width : cells + width, 2 * c : 4 * c]))
+    sums[starts.skip_weight : starts.skip_weight + 2 * c, :] = fold_rows(part)
+    small_row(3, total_cot)
+    begin()
+
     result = scratch.result
     last_bias = inputs.dec_conv2_bias[...] + inputs.skip_bias[...]
 
@@ -1279,79 +1356,10 @@
     )
     output_swap.first()
 
-    exchanges = []
-    waiting_runs = list(runs)
-    landing_at = 0
-    sem_at = 3 * (line - 1) + 20
-    sums = scratch.sums
-
-    def begin():
-        nonlocal landing_at, sem_at
-        start, rows = waiting_runs.pop(0)
-        kind = Exchange if waiting_runs else SmallExchange
-        exchange = kind(place, start, rows, landing_at, sem_at)
-        landing_at += exchange.land_rows()
-        sem_at += exchange.count()
-        exchanges.append(exchange)
-        exchange.advance()
-
-    def advance(k):
-        exchange = exchanges[k]
-        exchange.advance()
-
-    due = list(DUE)
-
-    def point():
-        for k in due.pop(0):
-            advance(k)
-
-    def small_row(k, value):
-        sums[small_at + k : small_at + k + 1, :] = value
-
-    def spread_grad(source):
-        def step(h, carry):
-            value = source[row_at(h), :]
-            put_row(scratch.xg, h, value)
-            return carry + tile_sums(value)
-
-        return grid_rows(step, zeros8)
-
-    def weight_grad(turned, at, depth, a):
-        rows = pl.ds((2 - a) * width, cells)
-        both = dot(turned[...], scratch.xg[rows, :])
-        for half in range(depth // c):
-            part = fold_rows(both[2 * c * half : 2 * c * (half + 1)])
-            for b in range(3):
-                high, low = HIGH_AT[2 - b] * c, LOW_AT[2 - b] * c
-                to = at + (3 * a + b) * depth + half * c
-                sums[to : to + c, :] = part[:, high : high + c] + part[:, low : low + c]
-
-    def back_conv(weight, slope, target, source, mean, inv):
-        carry = (zeros8, zeros8)
-        for i in range(cells // CHUNK):
-            value = fold(conv_chunk([(scratch.xg, weight)], i)) * slope[chunk_at(i), :]
-            target[chunk_at(i), :] = value
-            normed = (source[chunk_at(i), :] - mean) * inv
-            carry = (carry[0] + tile_sums(value), carry[1] + tile_sums(value * normed))
-            if i % (cells // CHUNK // 2) == cells // CHUNK // 2 - 1:
-                point()
-        return carry
-
-    def norm_grad(sums_in, scale, ones, count):
-        one, two = group_sums(sums_in[0] * scale, sums_in[1] * scale, ones)
-        return one / count, two / count
-
-    cot[here_rows] = cot_from[row]
-    cot_swap.arrive()
-    total_cot = column_sum(spread_grad(cot))
-    for a in range(3):
-        weight_grad(scratch.td2, starts.dec_conv2, c, a)
-    part = fold(dot(scratch.turned[...], scratch.xg[width : cells + width, 2 * c : 4 * c]))
-    sums[starts.skip_weight : starts.skip_weight + 2 * c, :] = fold_rows(part)
-    small_row(3, total_cot)
-    begin()
+    point()
 
     grad = scratch.grad
+    stack_turned(scratch.dec_conv2, 0, c, scratch.bd2)
     sums_d2 = back_conv(scratch.bd2, scratch.slope_d2, grad, middle_d, mean_d2, inv_d2)
     side_grads = (scratch.grad_a, scratch.grad_b)
     for half in range(2):
@@ -1388,13 +1396,14 @@
     small_row(9, bias_row)
     middle_grad(middle_d, mean_d2, inv_d2, gain_d2 * (1.0 + dec_scale), sums_d2)
     point()
-    output_swap.second()
     for a in range(3):
         weight_grad(scratch.td1, starts.dec_conv1, 2 * c, a)
         point()
         begin()
 
+    output_swap.second()
     for half, (source, mean, inv, gain) in enumerate(halves):
+        stack_turned(scratch.dec_conv1, half, 2 * c, (scratch.bd1a, scratch.bd1b)[half])
         sums_in = back_conv(
             (scratch.bd1a, scratch.bd1b)[half],
             (scratch.slope_d1a, scratch.slope_d1b)[half],
@@ -1420,7 +1429,6 @@
             small_row(2, column_sum(total))
         point()
 
-    output_swap.third()
     grad_raised, grad_encoded = side_grads
     x_grad_up = scratch.x_grad_up
     for k, piece in enumerate(pick(grad_raised)):
@@ -1446,6 +1454,7 @@
         grad, [fold(dot(x_grad_low[...], scratch.b_down[k])) for k in range(4)]
     )
 
+    output_swap.third()
     def join_row(h, carry):
         value = grad_encoded[row_at(h), :] + grad[row_at(h), :]
         grad_encoded[row_at(h), :] = value
@@ -1461,6 +1470,7 @@
         weight_grad(scratch.te2, starts.enc_conv2, c, a)
         point()
     begin()
+    stack_turned(scratch.enc_conv2, 0, c, scratch.be2)
     sums_e2 = back_conv(scratch.be2, scratch.slope_e2, grad, middle_e, mean_e2, inv_e2)
     gain_row, bias_row = table_rows(LATE + 24, sums_e2, gain_e2, bias_e2, 1.0 + enc_scale)
     small_row(LATE + 18, gain_row)
@@ -1472,6 +1482,7 @@
         point()
         if a:
             begin()
+    stack_turned(scratch.enc_conv1, 0, c, scratch.be1)
     sums_e1 = back_conv(scratch.be1, scratch.slope_e1, grad, lifted, mean_e1, inv_e1)
     small_row(LATE + 16, column_sum(sums_e1[1]))
     small_row(LATE + 17, column_sum(sums_e1[0]))

time: 90.5 us -> 92.3 us (1.020)
  Pallas kernels: 89.5 us -> 91.3 us
    pallas_call x1, Pallas kernels: 86.7 us -> 88.5 us  [whole_items(): pl.pallas_call(functools.partial(item_kernel, (line, strip, width, shapes...]
where the time goes in v1:
time: 92.3 us; the launch traced here: 92.1 us
  Pallas kernels  91.3 us (99%)
    pallas_call x1, Pallas kernels, whole_items(): pl.pallas_call(functools.partial(item_kernel, (line, strip, width, shapes...  88.5 us
    pallas_call x1, Pallas kernels, whole_items(): pl.pallas_call(functools.partial(write_kernel, (shapes, starts, small_at)...  2.75 us

profile of v1, /device:TPU:1, one launch (start us, length us, event | category | flops | bytes accessed | tf_op | source)
XLA Modules:
  0.0 92.1 jit_solution(8936385998390026775)
XLA Ops:
  0.7 88.5 %shard_map.476 = (f32[4,256,128]{2,1,0:T(8,128)S(1)}, f32[4,12,4,64]{3,2,1,0:T(4,128)S(1)}, f32[7136,128]{1,0:T(8,128)S(1)}) custom-call(f32[4,12,4,64]{3,2,1,0:T(4,128)} %refs_0_.1, s32[4]{0:T(128)} %refs_1_.1, s32[4,4,64]{2,1,0:T(4,128)} %refs_2_.1, s32[4]{0:T(128)} %refs_3_.1, f32[12,128]{1,0:T(8,128)} %refs_4_.1, f32[1,128]{1,0:T(1,128)} %bitcast.51, ...), custom_call_target="tpu_custom_call" | custom-call | tf_op jit(solution)/shard_map/pallas_call | solution.py:1677
  89.2 2.8 %shard_map.477 = (f32[4,256,128]{2,1,0:T(8,128)}, f32[4,12,4,64]{3,2,1,0:T(4,128)}, f32[2304,128]{1,0:T(8,128)}, f32[512,128]{1,0:T(8,128)}, f32[512,128]{1,0:T(...) custom-call(f32[4,256,128]{2,1,0:T(8,128)S(1)} %get-tuple-element.55, ...), custom_call_target="tpu_custom_call" | custom-call | tf_op jit(solution)/shard_map/pallas_call | solution.py:1692
